TPU v7x, 128 devices: a whole 4x4x4 slice. The times are simulated.
128 devices in a mesh: gx: 8 (over z_hi, x), gy: 16 (over y, z_lo, core).
Axes of the slice: x: 4, y: 4, z: 4 (z_hi: 2, z_lo: 2; z = z_hi * 2 + z_lo), core: 2. Of those that a mesh axis runs over, the one named last changes fastest.
Arguments:
- inputs: bfloat16 [1024, 8192], P('gx', 'gy'), may hold values from -6 to 6
- out_grad: bfloat16 [1024, 8192], P('gx', 'gy'), may hold values from -1.1953125 to 1.1953125
- pre_act: bfloat16 [1024, 32768], P('gy', 'gx'), may hold values from -6 to 6
- w_in: bfloat16 [8192, 32768], P('gy', 'gx'), may hold values from -0.0625 to 0.0625
- w_out: bfloat16 [32768, 8192], P('gx', 'gy'), may hold values from -0.03125 to 0.03125
- counts: int32 [8], replicated, may hold values from 1 to 128, 640 in all
Outputs:
- in_grad: bfloat16 [1024, 8192], P('gx', 'gy')
- w_in_grad: bfloat16 [8192, 32768], P('gy', 'gx')
- w_out_grad: bfloat16 [32768, 8192], P('gx', 'gy')
Inputs may be any that keep to these rules, and one draw needn't show every extreme that they name: In batch shard s (token slots s * 128 to (s + 1) * 128 - 1) the first counts[s] slots are live and the rest are padding; the counts add up to exactly 640, and at least one shard is full.
All inputs are finite; a program needn't handle non-finite values.
Results may differ from a plain program's by a relative error of at most 0.0051.
Values may be sent and summed in bfloat16 or wider, within the bound.
A program may use at most 128 MiB of HBM per device.

v0:
```python
import math

import jax
import jax.numpy as jnp
from jax import lax
from jax.sharding import PartitionSpec as P

gelu_scale = math.sqrt(2.0 / math.pi)
cubic_coef = 0.044715


def gelu_value(pre):
    tangent = jnp.tanh(gelu_scale * (pre + cubic_coef * pre * pre * pre))
    return 0.5 * pre * (1.0 + tangent)


def gelu_slope(pre):
    tangent = jnp.tanh(gelu_scale * (pre + cubic_coef * pre * pre * pre))
    return 0.5 * (1.0 + tangent) + 0.5 * pre * (1.0 - tangent * tangent) * gelu_scale * (
        1.0 + 3.0 * cubic_coef * pre * pre
    )


def token_sum(left, right):
    return lax.dot_general(
        left, right, (((0,), (0,)), ((), ())), preferred_element_type=jnp.float32
    )


def contract_last(left, right):
    return lax.dot_general(
        left, right, (((1,), (1,)), ((), ())), preferred_element_type=jnp.float32
    )


def live_mask(counts, shard_rows, all_rows, shards):
    positions = jnp.arange(all_rows, dtype=jnp.int32)
    owner_shard = positions // shard_rows
    one_hot = owner_shard[:, None] == jnp.arange(shards, dtype=jnp.int32)[None, :]
    own_count = jnp.sum(jnp.where(one_hot, counts[None, :], 0), axis=1)
    return positions % shard_rows < own_count


def body(inputs, out_grad, pre_act, w_in, w_out, counts):
    shard_rows = inputs.shape[0]
    shards = lax.axis_size("gx")
    all_rows = shard_rows * shards
    gathered_x, gathered_dy = (
        lax.all_gather(inputs, "gx", axis=0, tiled=True),
        lax.all_gather(out_grad, "gx", axis=0, tiled=True),
    )
    is_live = live_mask(counts, shard_rows, all_rows, shards)
    masked_grad = jnp.where(is_live[:, None], gathered_dy, jnp.zeros_like(gathered_dy))
    whole_pre = lax.all_gather(pre_act, "gy", axis=0, tiled=True).astype(jnp.float32)
    activation = gelu_value(whole_pre).astype(jnp.bfloat16)
    hidden_total = lax.psum(contract_last(masked_grad, w_out), "gy")
    sent_hidden = (hidden_total * gelu_slope(whole_pre)).astype(jnp.bfloat16)
    w_out_grad = token_sum(activation, masked_grad)
    w_in_grad = token_sum(gathered_x, sent_hidden)
    in_part = lax.psum_scatter(
        contract_last(sent_hidden, w_in), "gx", scatter_dimension=0, tiled=True
    )
    return (
        in_part.astype(jnp.bfloat16),
        w_in_grad.astype(jnp.bfloat16),
        w_out_grad.astype(jnp.bfloat16),
    )


def solution(mesh):
    return jax.shard_map(
        body,
        mesh=mesh,
        in_specs=(P("gx", "gy"), P("gx", "gy"), P("gy", "gx"), P("gy", "gx"), P("gx", "gy"), P()),
        out_specs=(P("gx", "gy"), P("gy", "gx"), P("gx", "gy")),
        check_vma=False,
    )
```

profile of v0, /device:TPU:1, one launch (start us, length us, event | category | flops | bytes accessed | tf_op | source)
XLA Modules:
  0.0 614.0 jit_solution(13120860873602182019)
XLA Ops:
  7.2 0.0 all-gather.4.cloned.1.call-start
  7.2 0.7 all-gather.4.cloned.1.call-update
  7.9 0.0 all-gather.6.cloned.1.call-start
  7.9 0.7 all-gather.6.cloned.1.call-update
  8.6 0.0 all-reduce.2.cloned.1.call-start
  8.7 0.7 select_reduce_fusion
  9.5 50.6 %all-gather.4.cloned.1.call-done = bf16[1024,512]{1,0:T(8,128)(2,1)} async-done(((bf16[128,512]{1,0:T(8,128)(2,1)}), bf16[1024,512]{1,0:T(8,128)(2,1)}) %all-gather.4.cloned.1.call-update) | async-done | bytes 1048592 | tf_op jit(solution)/shard_map/all_gather | solution.py:50
  60.0 13.0 %fusion.17 = f32[1024,4096]{1,0:T(8,128)} fusion(bf16[4096,512]{1,0:T(8,128)(2,1)} %param.10, bf16[1024,512]{1,0:T(8,128)(2,1)} %all-gather.4.cloned.1.call-done, pred[1024]{0:T(1024)(128)(4,1)S(1)} %fusion.18), kind=kOutput, calls=%fused_computation.23 | convolution fusion | flops 4295491584 | bytes 22021120 | tf_op jit(solution)/shard_map/dot_general | solution.py:31
  73.0 0.0 all-reduce.2.cloned.1.call-update
  73.0 0.0 all-gather.8.cloned.1.call-start
  73.1 0.5 all-gather.8.cloned.1.call-update
  73.6 0.2 reduce-scatter.2.cloned.1.call-start
  73.8 40.1 %all-gather.6.cloned.1.call-done = bf16[1024,4096]{1,0:T(8,128)(2,1)} async-done(((bf16[64,4096]{1,0:T(8,128)(2,1)}), bf16[1024,4096]{1,0:T(8,128)(2,1)}) %all-gather.6.cloned.1.call-update) | async-done | bytes 8388624 | tf_op jit(solution)/shard_map/all_gather | solution.py:54
  113.9 365.3 %all-reduce.2.cloned.1.call-done = f32[1024,4096]{1,0:T(8,128)} async-done(((f32[1024,4096]{1,0:T(8,128)}), f32[1024,4096]{1,0:T(8,128)}) %all-reduce.2.cloned.1.call-update) | async-done | bytes 16777232 | tf_op jit(solution)/shard_map/psum | solution.py:56
  479.2 14.2 %fusion.6 = bf16[1024,4096]{1,0:T(8,128)(2,1)S(1)} fusion(f32[1024,4096]{1,0:T(8,128)} %all-reduce.2.cloned.1.call-done, bf16[1024,4096]{1,0:T(8,128)(2,1)} %all-gather.6.cloned.1.call-done), kind=kLoop, calls=%fused_computation.13 | loop fusion | flops 83886080 | bytes 33554432 | tf_op jit(solution)/shard_map/convert_element_type | solution.py:57
  493.5 3.2 copy-done
  496.7 5.8 fusion.30
  502.5 0.0 reduce-scatter.2.cloned.1.call-update
  502.6 11.8 %fusion.13 = bf16[4096,512]{1,0:T(8,128)(2,1)} fusion(bf16[1024,4096]{1,0:T(8,128)(2,1)} %all-gather.6.cloned.1.call-done, bf16[1024,512]{1,0:T(8,128)(2,1)S(1)} %copy-done.2, pred[1024]{0:T(1024)(128)(4,1)S(1)} %fusion.18), kind=kOutput, calls=%fused_computation.20 | convolution fusion | flops 4339531776 | bytes 13632512 | tf_op jit(solution)/shard_map/dot_general | solution.py:25
  514.3 14.3 %all-gather.8.cloned.1.call-done = bf16[1024,512]{1,0:T(8,128)(2,1)} async-done(((bf16[128,512]{1,0:T(8,128)(2,1)}), bf16[1024,512]{1,0:T(8,128)(2,1)}) %all-gather.8.cloned.1.call-update) | async-done | bytes 1048592 | tf_op jit(solution)/shard_map/all_gather | solution.py:49
  528.6 10.2 %fusion.16 = bf16[512,4096]{0,1:T(8,128)(2,1)} fusion(bf16[1024,4096]{1,0:T(8,128)(2,1)} %copy-done, bf16[1024,512]{1,0:T(8,128)(2,1)} %all-gather.8.cloned.1.call-done), kind=kOutput, calls=%fused_computation.21 | convolution fusion | flops 4297064448 | bytes 13631488 | tf_op jit(solution)/shard_map/dot_general | solution.py:25
  538.8 6.4 %copy.10 = bf16[512,4096]{1,0:T(8,128)(2,1)} copy(bf16[512,4096]{0,1:T(8,128)(2,1)} %fusion.16) | data formatting | bytes 8388608
  545.2 60.7 %reduce-scatter.2.cloned.1.call-done = f32[128,512]{1,0:T(8,128)} async-done(((f32[1024,512]{1,0:T(8,128)}), f32[128,512]{1,0:T(8,128)}) %reduce-scatter.2.cloned.1.call-update) | async-done | bytes 262160 | tf_op jit(solution)/shard_map/reduce_scatter | solution.py:60
  605.9 1.6 convert_element_type.23
  (7 shorter events, 0.0 us)
Async XLA Ops:
  7.2 52.9 %all-gather.4.cloned.1.call-start = ((), (), s32[]{:S(2)}) async-start(), calls=%async_computation.1 | async-start | bytes 1179648 | tf_op jit(solution)/shard_map/all_gather | solution.py:50
  7.9 106.0 %all-gather.6.cloned.1.call-start = ((), (), s32[]{:S(2)}) async-start(), calls=%async_computation.3 | async-start | bytes 8912896 | tf_op jit(solution)/shard_map/all_gather | solution.py:54
  8.6 470.6 %all-reduce.2.cloned.1.call-start = ((), (), s32[]{:S(2)}) async-start(), calls=%async_computation.2 | async-start | bytes 33554432 | tf_op jit(solution)/shard_map/psum | solution.py:56
  73.0 455.6 %all-gather.8.cloned.1.call-start = ((), (), s32[]{:S(2)}) async-start(), calls=%async_computation.5 | async-start | bytes 1179648 | tf_op jit(solution)/shard_map/all_gather | solution.py:49
  73.6 532.3 %reduce-scatter.2.cloned.1.call-start = ((), (), s32[]{:S(2)}) async-start(), calls=%async_computation.4 | async-start | bytes 2359296 | tf_op jit(solution)/shard_map/reduce_scatter | solution.py:60
  479.2 17.5 %copy-start.1 = (bf16[512,4096]{1,0:T(8,128)(2,1)S(1)}, bf16[512,4096]{1,0:T(8,128)(2,1)}, u32[]{:S(2)}) copy-start(bf16[512,4096]{1,0:T(8,128)(2,1)} %param.9) | copy-start | bytes 12582916
  493.4 3.2 copy-start
  496.7 5.9 copy-start.2
Sparse Core Ops, SparseCore 0:
  10.3 49.6 all-gather.3
  61.7 52.1 all-gather.5
  116.5 362.7 all-reduce.1
  481.4 47.1 all-gather.7
  532.3 73.5 reduce-scatter.1
where the time goes:
time: 615 us; the launch traced here: 614 us
  waiting for transfers between devices  533 us (87%)
  matrix products  40.8 us (7%)
  other arithmetic  16.6 us (3%)
  between operations  13.8 us (2%)
  local copies, waits for them, and re-layouts  9.59 us (2%)
    psum x1, waiting for transfers between devices, body(): hidden_total = lax.psum(contract_last(masked_grad, w_out), 'gy')  365 us
    reduce_scatter x1, waiting for transfers between devices, body(): lax.psum_scatter(contract_last(sent_hidden, w_in), 'gx', scatter_dimensio...  60.7 us
    all_gather x1, waiting for transfers between devices, body(): lax.all_gather(out_grad, 'gx', axis=0, tiled=True)  50.6 us
    all_gather x1, waiting for transfers between devices, body(): lax.all_gather(pre_act, 'gy', axis=0, tiled=True).astype(jnp.float32)  40.1 us
    dot_general x2, matrix products, token_sum(): lax.dot_general(left, right, (((0,), (0,)), ((), ())), preferred_element_...  21.9 us
    dot_general x2, matrix products, contract_last(): lax.dot_general(left, right, (((1,), (1,)), ((), ())), preferred_element_...  18.8 us
    all_gather x1, waiting for transfers between devices, body(): lax.all_gather(inputs, 'gx', axis=0, tiled=True)  14.3 us
    convert_element_type x1, other arithmetic, body(): sent_hidden = (hidden_total * gelu_slope(whole_pre)).astype(jnp.bfloat16)  14.2 us
  transfers between devices with their start and end apart: 5, of which 5 were waited for; matrix products, arithmetic and copies ran while one was open for 10% of the time, Pallas kernels for 0%

commit v1 on v0

v1 whole, which is shorter than its diff:
```python
import math

import jax
import jax.numpy as jnp
from jax import lax
from jax.sharding import PartitionSpec as P

LIVE = 640
gelu_scale = math.sqrt(2.0 / math.pi)
cubic_coef = 0.044715


def gelu_parts(pre):
    tangent = jnp.tanh(gelu_scale * (pre + cubic_coef * pre * pre * pre))
    value = 0.5 * pre * (1.0 + tangent)
    slope = 0.5 * (1.0 + tangent) + 0.5 * pre * (1.0 - tangent * tangent) * gelu_scale * (
        1.0 + 3.0 * cubic_coef * pre * pre
    )
    return value, slope


def token_sum(left, right):
    return lax.dot_general(
        left, right, (((0,), (0,)), ((), ())), preferred_element_type=jnp.float32
    )


def contract_last(left, right):
    return lax.dot_general(
        left, right, (((1,), (1,)), ((), ())), preferred_element_type=jnp.float32
    )


def pick_matrix(counts, shard_rows, all_rows, shards):
    token = jnp.arange(all_rows, dtype=jnp.int32)
    shard = jnp.arange(shards, dtype=jnp.int32)
    starts = jnp.sum(jnp.where(shard[None, :] < shard[:, None], counts[None, :], 0), axis=1)
    owner = token // shard_rows
    one_hot = owner[:, None] == jnp.arange(shards, dtype=jnp.int32)[None, :]
    own_count = jnp.sum(jnp.where(one_hot, counts[None, :], 0), axis=1)
    own_start = jnp.sum(jnp.where(one_hot, starts[None, :], 0), axis=1)
    slot = token % shard_rows
    place = jnp.where(slot < own_count, own_start + slot, -1)
    return (place[None, :] == jnp.arange(LIVE, dtype=jnp.int32)[:, None]).astype(jnp.bfloat16)


def body(inputs, out_grad, pre_act, w_in, w_out, counts):
    shard_rows = inputs.shape[0]
    shards = lax.axis_size("gx")
    all_rows = shard_rows * shards
    pick = pick_matrix(counts, shard_rows, all_rows, shards)

    def compact(whole):
        return jnp.dot(pick, whole, preferred_element_type=jnp.float32).astype(whole.dtype)

    live_dy = compact(lax.all_gather(out_grad, "gx", axis=0, tiled=True))
    live_x = compact(lax.all_gather(inputs, "gx", axis=0, tiled=True))
    my_pre = lax.all_to_all(pre_act, "gy", split_axis=1, concat_axis=0, tiled=True)
    value, slope = gelu_parts(compact(my_pre).astype(jnp.float32))
    activation = lax.all_gather(value.astype(jnp.bfloat16), "gy", axis=1, tiled=True)
    hidden = lax.psum_scatter(
        contract_last(live_dy, w_out), "gy", scatter_dimension=1, tiled=True
    )
    hidden_grad = lax.all_gather(
        (hidden * slope).astype(jnp.bfloat16), "gy", axis=1, tiled=True
    )
    w_out_grad = token_sum(activation, live_dy)
    w_in_grad = token_sum(live_x, hidden_grad)
    part = contract_last(hidden_grad, w_in)
    spread = lax.dot_general(
        pick, part.astype(jnp.bfloat16), (((0,), (0,)), ((), ())), preferred_element_type=jnp.float32
    )
    in_part = lax.psum_scatter(spread, "gx", scatter_dimension=0, tiled=True)
    return (
        in_part.astype(jnp.bfloat16),
        w_in_grad.astype(jnp.bfloat16),
        w_out_grad.astype(jnp.bfloat16),
    )


def solution(mesh):
    return jax.shard_map(
        body,
        mesh=mesh,
        in_specs=(P("gx", "gy"), P("gx", "gy"), P("gy", "gx"), P("gy", "gx"), P("gx", "gy"), P()),
        out_specs=(P("gx", "gy"), P("gy", "gx"), P("gx", "gy")),
        check_vma=False,
    )
```

time: 615 us -> 427 us (0.69)
  waiting for transfers between devices: 533 us -> 353 us
  blocking collectives: 0 us -> 17.3 us
  other arithmetic: 16.6 us -> 3.15 us
  local copies, waits for them, and re-layouts: 9.59 us -> 1.28 us
    psum x1 -> x0, waiting for transfers between devices: 365 us -> none  [body(): hidden_total = lax.psum(contract_last(masked_grad, w_out), 'gy')]
    reduce_scatter x1 -> x2, waiting for transfers between devices: 60.7 us -> 171 us  [the longest x1 103 us: body(): lax.psum_scatter(contract_last(live_dy, w_out), 'gy', scatter_dimension=1...]
    all_gather x3 -> x4, waiting for transfers between devices: 105 us -> 180 us  [the longest x1 50.6 us: body(): live_dy = compact(lax.all_gather(out_grad, 'gx', axis=0, tiled=True))]
    all_to_all x0 -> x1, blocking collectives: none -> 17.3 us  [body(): lax.all_to_all(pre_act, 'gy', split_axis=1, concat_axis=0, tiled=True)]
    convert_element_type x1 -> x0, other arithmetic: 14.2 us -> none  [body(): sent_hidden = (hidden_total * gelu_slope(whole_pre)).astype(jnp.bfloat16)]
    dot_general x0 -> x3, matrix products: none -> 13.9 us  [the longest x1 8.83 us: body(): lax.dot_general(pick, part.astype(jnp.bfloat16), (((0,), (0,)), ((), ()))...]
    dot_general x2 -> x1, matrix products: 18.8 us -> 5.47 us  [contract_last(): lax.dot_general(left, right, (((1,), (1,)), ((), ())), preferred_element_...]
    unnamed x7 -> x4, local copies, waits for them, and re-layouts: 9.59 us -> 1.24 us
  transfers between devices with their start and end apart: 5 -> 6, of which waited for: 5 -> 6; matrix products, arithmetic and copies ran while one was open for 10% -> 6% of each run, Pallas kernels for 0% -> 0%
where the time goes in v1:
time: 427 us; the launch traced here: 426 us
  waiting for transfers between devices  353 us (83%)
  matrix products  35.9 us (8%)
  blocking collectives  17.3 us (4%)
  between operations  14.1 us (3%)
    reduce_scatter x1, waiting for transfers between devices, body(): lax.psum_scatter(contract_last(live_dy, w_out), 'gy', scatter_dimension=1...  103 us
    reduce_scatter x1, waiting for transfers between devices, body(): in_part = lax.psum_scatter(spread, 'gx', scatter_dimension=0, tiled=True)  68.3 us
    all_gather x1, waiting for transfers between devices, body(): live_dy = compact(lax.all_gather(out_grad, 'gx', axis=0, tiled=True))  50.6 us
    all_gather x1, waiting for transfers between devices, body(): lax.all_gather((hidden * slope).astype(jnp.bfloat16), 'gy', axis=1, tiled...  48.7 us
    all_gather x1, waiting for transfers between devices, body(): lax.all_gather(value.astype(jnp.bfloat16), 'gy', axis=1, tiled=True)  41.8 us
    all_gather x1, waiting for transfers between devices, body(): live_x = compact(lax.all_gather(inputs, 'gx', axis=0, tiled=True))  39.2 us
    all_to_all x1, blocking collectives, body(): lax.all_to_all(pre_act, 'gy', split_axis=1, concat_axis=0, tiled=True)  17.3 us
    dot_general x2, matrix products, token_sum(): lax.dot_general(left, right, (((0,), (0,)), ((), ())), preferred_element_...  16.6 us
  transfers between devices with their start and end apart: 6, of which 6 were waited for; matrix products, arithmetic and copies ran while one was open for 6% of the time, Pallas kernels for 0%

profile of v1, /device:TPU:1, one launch (start us, length us, event | category | flops | bytes accessed | tf_op | source)
XLA Modules:
  0.0 425.7 jit_solution(5005379387984261748)
XLA Ops:
  7.2 0.7 all-gather.5.cloned.1.call-update
  8.0 0.8 select_reduce_fusion.2
  8.7 0.7 select_reduce_fusion.1
  9.5 50.6 %all-gather.5.cloned.1.call-done = bf16[1024,512]{1,0:T(8,128)(2,1)} async-done(((bf16[128,512]{1,0:T(8,128)(2,1)}), bf16[1024,512]{1,0:T(8,128)(2,1)}) %all-gather.5.cloned.1.call-update) | async-done | bytes 1048592 | tf_op jit(solution)/shard_map/all_gather | solution.py:56
  60.0 2.2 fusion.4
  62.3 0.3 copy-done.1
  62.5 5.5 %fusion.28 = f32[640,4096]{1,0:T(8,128)} fusion(bf16[640,512]{1,0:T(8,128)(2,1)S(1)} %fusion.4, bf16[4096,512]{1,0:T(8,128)(2,1)S(1)} %copy-done.1), kind=kOutput, calls=%fused_computation.51 | convolution fusion | flops 2684354560 | bytes 15335424 | tf_op jit(solution)/shard_map/dot_general | solution.py:29
  68.0 0.0 all-gather.7.cloned.1.call-start
  68.1 1.0 copy-done
  69.1 17.3 %all_to_all.19 = bf16[64,16,256]{2,0,1:T(8,128)(2,1)S(1)} all-to-all(bf16[64,16,256]{2,0,1:T(8,128)(2,1)S(1)} %bitcast.17), channel_id=1, replica_groups=mesh['gx'=8,'gy'=16] {'gy'}, dimensions={1} | all-to-all | bytes 1048576 | tf_op jit(solution)/shard_map/all_to_all | solution.py:58
  86.4 103.1 %reduce-scatter.3.cloned.1.call-done = f32[640,256]{1,0:T(8,128)} async-done(((f32[640,4096]{1,0:T(8,128)}), f32[640,256]{1,0:T(8,128)}) %reduce-scatter.3.cloned.1.call-update) | async-done | bytes 655376 | tf_op jit(solution)/shard_map/reduce_scatter | solution.py:61
  189.5 2.8 fusion.18
  192.4 0.0 all-gather.11.cloned.1.call-start
  192.4 0.5 all-gather.11.cloned.1.call-update
  193.0 0.5 all-gather.9.cloned.1.call-update
  193.5 0.2 reduce-scatter.5.cloned.1.call-start
  193.8 48.7 %all-gather.7.cloned.1.call-done = bf16[640,4096]{1,0:T(8,128)(2,1)} async-done(((bf16[640,256]{1,0:T(8,128)(2,1)}), bf16[640,4096]{1,0:T(8,128)(2,1)}) %all-gather.7.cloned.1.call-update) | async-done | bytes 5242896 | tf_op jit(solution)/shard_map/all_gather | solution.py:64
  242.4 8.8 %fusion.1 = f32[1024,512]{1,0:T(8,128)} fusion(s32[1024]{0:T(1024)S(1)} %add_select_fusion.2, bf16[640,4096]{1,0:T(8,128)(2,1)} %all-gather.7.cloned.1.call-done, bf16[512,4096]{1,0:T(8,128)(2,1)} %param.9), kind=kOutput, calls=%fused_computation.4 | convolution fusion | flops 3356426240 | bytes 11538432 | tf_op jit(solution)/shard_map/dot_general | solution.py:70
  251.3 41.8 %all-gather.11.cloned.1.call-done = bf16[640,4096]{1,0:T(8,128)(2,1)} async-done(((bf16[640,256]{1,0:T(8,128)(2,1)}), bf16[640,4096]{1,0:T(8,128)(2,1)}) %all-gather.11.cloned.1.call-update) | async-done | bytes 5242896 | tf_op jit(solution)/shard_map/all_gather | solution.py:60
  293.1 7.6 %convolution_convert_fusion = bf16[4096,512]{1,0:T(8,128)(2,1)} fusion(bf16[640,4096]{1,0:T(8,128)(2,1)} %all-gather.11.cloned.1.call-done, bf16[640,512]{1,0:T(8,128)(2,1)S(1)} %fusion.4), kind=kOutput, calls=%fused_computation | convolution fusion | flops 2686451712 | bytes 10092544 | tf_op jit(solution)/shard_map/dot_general | solution.py:23
  300.6 39.2 %all-gather.9.cloned.1.call-done = bf16[1024,512]{1,0:T(8,128)(2,1)} async-done(((bf16[128,512]{1,0:T(8,128)(2,1)}), bf16[1024,512]{1,0:T(8,128)(2,1)}) %all-gather.9.cloned.1.call-update) | async-done | bytes 1048592 | tf_op jit(solution)/shard_map/all_gather | solution.py:57
  339.8 9.1 %convolution_convert_fusion.1 = bf16[512,4096]{1,0:T(8,128)(2,1)} fusion(bf16[640,4096]{1,0:T(8,128)(2,1)} %all-gather.7.cloned.1.call-done, bf16[1024,512]{1,0:T(8,128)(2,1)} %all-gather.9.cloned.1.call-done, s32[1024]{0:T(1024)S(1)} %add_select_fusion.2), kind=kOutput, calls=%fused_computation.1 | convolution fusion | flops 3358523392 | bytes 10489856 | tf_op jit(solution)/shard_map/dot_general | solution.py:23
  348.9 68.3 %reduce-scatter.5.cloned.1.call-done = f32[128,512]{1,0:T(8,128)} async-done(((f32[1024,512]{1,0:T(8,128)}), f32[128,512]{1,0:T(8,128)}) %reduce-scatter.5.cloned.1.call-update) | async-done | bytes 262160 | tf_op jit(solution)/shard_map/reduce_scatter | solution.py:73
  417.2 1.6 convert_element_type.36
  (11 shorter events, 0.2 us)
Async XLA Ops:
  7.2 52.9 %all-gather.5.cloned.1.call-start = ((), (), s32[]{:S(2)}) async-start(), calls=%async_computation.3 | async-start | bytes 1179648 | tf_op jit(solution)/shard_map/all_gather | solution.py:56
  7.9 181.6 %reduce-scatter.3.cloned.1.call-start = ((), (), s32[]{:S(2)}) async-start(), calls=%async_computation.4 | async-start | bytes 11141120 | tf_op jit(solution)/shard_map/reduce_scatter | solution.py:61
  60.0 2.5 copy-start.1
  68.0 1.0 copy-start
  68.0 174.4 %all-gather.7.cloned.1.call-start = ((), (), s32[]{:S(2)}) async-start(), calls=%async_computation.5 | async-start | bytes 5570560 | tf_op jit(solution)/shard_map/all_gather | solution.py:64
  192.4 100.7 %all-gather.11.cloned.1.call-start = ((), (), s32[]{:S(2)}) async-start(), calls=%async_computation.8 | async-start | bytes 5570560 | tf_op jit(solution)/shard_map/all_gather | solution.py:60
  193.0 146.9 %all-gather.9.cloned.1.call-start = ((), (), s32[]{:S(2)}) async-start(), calls=%async_computation.7 | async-start | bytes 1179648 | tf_op jit(solution)/shard_map/all_gather | solution.py:57
  193.5 223.6 %reduce-scatter.5.cloned.1.call-start = ((), (), s32[]{:S(2)}) async-start(), calls=%async_computation.6 | async-start | bytes 2359296 | tf_op jit(solution)/shard_map/reduce_scatter | solution.py:73
Sparse Core Ops, SparseCore 0:
  10.3 49.6 all-gather.4
  68.2 121.3 reduce-scatter.2
  192.5 49.8 all-gather.6
  244.5 48.5 all-gather.10
  295.2 44.5 all-gather.8
  343.5 73.6 reduce-scatter.4

commit v2 on v1

v2 whole, which is shorter than its diff:
```python
import math

import jax
import jax.numpy as jnp
from jax import lax
from jax.experimental import pallas as pl
from jax.experimental.pallas import tpu as pltpu
from jax.sharding import PartitionSpec as P

LIVE = 640
SHARDS = 8
ROWS = 128
FEAT = 512
PIECES = 16
UNITS = 256
HA = 128
HB = UNITS - HA
MESH = pl.DeviceIdType.MESH
BF16, F32 = jnp.bfloat16, jnp.float32

gelu_scale = math.sqrt(2.0 / math.pi)
cubic_coef = 0.044715


def gelu_parts(pre):
    tangent = jnp.tanh(gelu_scale * (pre + cubic_coef * pre * pre * pre))
    value = 0.5 * pre * (1.0 + tangent)
    slope = 0.5 * (1.0 + tangent) + 0.5 * pre * (1.0 - tangent * tangent) * gelu_scale * (
        1.0 + 3.0 * cubic_coef * pre * pre
    )
    return value, slope


def dot(left, right, left_dim, right_dim):
    return lax.dot_general(
        left, right, (((left_dim,), (right_dim,)), ((), ())), preferred_element_type=F32
    )


def kernel(
    counts, x_ref, dy_ref, pre_ref, w_in_ref, w_out_ref,
    in_out, wi_out, wo_out,
    pt, dyg, xg, preg, dyt, dys, xt, wo_own, wo_sib, wi, act, hg, slope,
    held, part, rz_a, rz_b, ry_a, ry_b, acc, accb, in_send, in_recv, wig, wog,
    send_sem, recv_sem, local_sem,
):
    gx, gy = lax.axis_index("gx"), lax.axis_index("gy")
    x, zh = gx % 4, gx // 4
    core, z, y = gy % 2, (gy // 2) % 2, gy // 4

    def on_gy(dy, dz, dc=0):
        return ((y + dy) % 4) * 4 + ((z + dz) % 2) * 2 + (core + dc) % 2

    def on_gx(dx, dzh):
        return ((zh + dzh) % 2) * 4 + (x + dx) % 4

    YP, YM, Z, C = (gx, on_gy(1, 0)), (gx, on_gy(3, 0)), (gx, on_gy(0, 1)), (gx, on_gy(0, 0, 1))
    XP, XM, ZH = (on_gx(1, 0), gy), (on_gx(3, 0), gy), (on_gx(0, 1), gy)

    count = [0, 0]
    sent, stored = [], []

    def send(src, dst, device):
        k = count[0]
        count[0] += 1
        copy = pltpu.make_async_remote_copy(
            src_ref=src, dst_ref=dst, send_sem=send_sem.at[k], recv_sem=recv_sem.at[k],
            device_id=device, device_id_type=MESH,
        )
        copy.start()
        sent.append(copy)
        return copy

    def local(src, dst):
        k = count[1]
        count[1] += 1
        copy = pltpu.make_async_copy(src, dst, local_sem.at[k])
        copy.start()
        return copy

    own_pre = local(pre_ref.at[:, pl.ds(pl.multiple_of(gy * UNITS, UNITS), UNITS)], preg.at[gy])
    load_wo = local(w_out_ref.at[:, core], wo_own)
    load_wi = local(w_in_ref, wi)
    barrier = pltpu.get_barrier_semaphore()
    for d in range(1, PIECES):
        pl.semaphore_signal(barrier, inc=1, device_id=(gx, (gy + d) % PIECES), device_id_type=MESH)
    for d in range(1, SHARDS):
        pl.semaphore_signal(barrier, inc=1, device_id=((gx + d) % SHARDS, gy), device_id_type=MESH)

    start = jnp.int32(0)
    for s in range(SHARDS):
        number = counts[s]

        def fill(i, carry, s=s, start=start, number=number):
            slot = lax.broadcasted_iota(jnp.int32, (16, LIVE), 0) + i * 16
            column = lax.broadcasted_iota(jnp.int32, (16, LIVE), 1)
            hit = (column == slot + start) & (slot < number)
            pt[pl.ds(pl.multiple_of(s * ROWS + i * 16, 16), 16), :] = jnp.where(hit, 1.0, 0.0).astype(BF16)
            return carry

        lax.fori_loop(0, ROWS // 16, fill, 0)
        start = start + number
    dyg[gx] = dy_ref[...]
    xg[gx] = x_ref[...]
    pl.semaphore_wait(barrier, PIECES - 1 + SHARDS - 1)

    lo, hi = pl.ds(0, ROWS // 2), pl.ds(ROWS // 2, ROWS // 2)

    def ring_start(src, buf):
        return send(src, buf.at[gx], ZH), send(src, buf.at[gx], XP), send(src, buf.at[gx], XM)

    def ring_relay(buf, first):
        def pass_on(dzh, to_right, to_left):
            to_right.wait_recv()
            came = on_gx(3, dzh)
            a = send(buf.at[came, lo], buf.at[came, lo], XP)
            to_left.wait_recv()
            came = on_gx(1, dzh)
            b = send(buf.at[came, hi], buf.at[came, hi], XM)
            return [a, b]

        across, right, left = first
        across.wait_recv()
        other = on_gx(0, 1)
        right2 = send(buf.at[other], buf.at[other], XP)
        left2 = send(buf.at[other], buf.at[other], XM)
        return pass_on(0, right, left) + pass_on(1, right2, left2)

    dy_first = ring_start(dy_ref, dyg)
    swap_wo = send(w_out_ref.at[:, 1 - core], wo_sib, C)
    pre_copies = []
    for d in range(1, PIECES):
        to = (gy + d) % PIECES
        columns = pl.ds(pl.multiple_of(to * UNITS, UNITS), UNITS)
        pre_copies.append(send(pre_ref.at[:, columns], preg.at[gy], (gx, to)))
    dy_last = ring_relay(dyg, dy_first)
    x_first = ring_start(x_ref, xg)

    def compact(buf, width):
        whole = buf[...].reshape(SHARDS * ROWS, width)
        return dot(whole, pt[...], 0, 0)

    for copy in dy_last:
        copy.wait_recv()
    dyt[...] = compact(dyg, FEAT).astype(BF16)
    swap_dy = send(dyt, dys, C)
    load_wo.wait()
    swap_wo.wait_recv()

    rows_a, rows_b = pl.ds(0, HA), pl.ds(HA, HB)
    QA, QB = HA // 2, HB // 2
    a0, a1, b0, b1 = pl.ds(0, QA), pl.ds(QA, QA), pl.ds(HA, QB), pl.ds(HA + QB, QB)
    ring = {}

    def ring_send(key, dy, dz, q0, q1, land):
        if dy == 2:
            ring[key, "relay+"] = send(part.at[dy, dz, q0], land.at[0], YP)
            ring[key, "relay-"] = send(part.at[dy, dz, q1], land.at[1], YM)
        if dy == 1:
            ring[key, "direct+"] = send(part.at[dy, dz, q1], land.at[2], YP)
        if dy == 3:
            ring[key, "direct-"] = send(part.at[dy, dz, q0], land.at[3], YM)

    def ring_pass(key, dz, q0, q1, land):
        ring[key, "relay+"].wait_recv()
        part[1, dz, q0, :] = (held[1, dz, q0, :] + land[0].astype(F32)).astype(BF16)
        ring[key, "last+"] = send(part.at[1, dz, q0], land.at[4], YP)
        ring[key, "relay-"].wait_recv()
        part[3, dz, q1, :] = (held[3, dz, q1, :] + land[1].astype(F32)).astype(BF16)
        ring[key, "last-"] = send(part.at[3, dz, q1], land.at[5], YM)

    def ring_total(key, dz, q0, q1, land):
        ring[key, "direct-"].wait_recv()
        ring[key, "last+"].wait_recv()
        total0 = held[0, dz, q0, :] + land[3].astype(F32) + land[4].astype(F32)
        ring[key, "direct+"].wait_recv()
        ring[key, "last-"].wait_recv()
        total1 = held[0, dz, q1, :] + land[2].astype(F32) + land[5].astype(F32)
        return total0, total1

    swap_dy.wait_recv()
    z_copies = {}
    for dy, dz in ((2, 1), (2, 0), (1, 1), (3, 1), (0, 1), (1, 0), (3, 0), (0, 0)):
        chip = ((y + dy) % 4) * 2 + (z + dz) % 2
        total = dot(wo_own[chip], dyt[...], 1, 0) + dot(wo_sib[chip], dys[...], 1, 0)
        held[dy, dz] = total
        part[dy, dz] = total.astype(BF16)
        ring_send(("a", dz), dy, dz, a0, a1, ry_a.at[dz])
        if dz == 1:
            z_copies[dy] = send(part.at[dy, dz, rows_b], rz_b.at[dy], Z)

    own_pre.wait()
    for copy in pre_copies:
        copy.wait_recv()
    slope[...] = dot(preg[...].reshape(SHARDS * ROWS, UNITS), pt[...], 0, 0)

    def gelu(i, carry):
        rows = pl.ds(pl.multiple_of(i * 16, 16), 16)
        value, tilt = gelu_parts(slope[rows, :])
        act[gy, rows, :] = value.astype(BF16)
        slope[rows, :] = tilt
        return carry

    lax.fori_loop(0, UNITS // 16, gelu, 0)

    for dz in (1, 0):
        ring_pass(("a", dz), dz, a0, a1, ry_a.at[dz])
    x_last = ring_relay(xg, x_first)
    for dy in (2, 1, 3, 0):
        z_copies[dy].wait_recv()
        total = held[dy, 0, rows_b, :] + rz_b[dy].astype(F32)
        held[dy, 0, rows_b, :] = total
        part[dy, 0, rows_b, :] = total.astype(BF16)
        ring_send("b", dy, 0, b0, b1, ry_b)
        if dy == 3:
            ring_pass("b", 0, b0, b1, ry_b)
    total0, total1 = ring_total(("a", 1), 1, a0, a1, ry_a.at[1])
    part[0, 1, a0, :] = total0.astype(BF16)
    part[0, 1, a1, :] = total1.astype(BF16)
    z_last = send(part.at[0, 1, rows_a], rz_a, Z)

    def gather_a(buf):
        own = buf.at[gy, rows_a]
        return {"z": send(own, own, Z), "+": send(own, own, YP), "-": send(own, own, YM), "c": send(own, own, C)}

    def gather_b(buf):
        own = buf.at[gy, rows_b]
        return {"+": send(own, own, YP), "-": send(own, own, YM), "z": send(own, own, Z), "c": send(own, own, C)}

    def gather_rest(buf, fa, fb, use):
        sib = {(0, 0): [fa["c"], fb["c"]]}

        def fwd(dy, dz, rows, device):
            piece = buf.at[on_gy(dy, dz), rows]
            return send(piece, piece, device)

        def to_sibling(dy, dz, rows):
            sib.setdefault((dy, dz), []).append(fwd(dy, dz, rows, C))

        def done(dy, dz):
            for copy in sib[dy, dz]:
                copy.wait_recv()
            use(((y + dy) % 4) * 2 + (z + dz) % 2)

        fa["z"].wait_recv()
        plus = fwd(0, 1, rows_a, YP)
        minus = fwd(0, 1, rows_a, YM)
        to_sibling(0, 1, rows_a)
        fa["+"].wait_recv()
        a20p = fwd(3, 0, a0, YP)
        to_sibling(3, 0, rows_a)
        fa["-"].wait_recv()
        a20m = fwd(1, 0, a1, YM)
        to_sibling(1, 0, rows_a)
        fb["+"].wait_recv()
        b20p = fwd(3, 0, b0, YP)
        zm = fwd(3, 0, rows_b, Z)
        to_sibling(3, 0, rows_b)
        fb["-"].wait_recv()
        b20m = fwd(1, 0, b1, YM)
        zp = fwd(1, 0, rows_b, Z)
        to_sibling(1, 0, rows_b)
        done(0, 0)
        plus.wait_recv()
        a21p = fwd(3, 1, a0, YP)
        to_sibling(3, 1, rows_a)
        minus.wait_recv()
        a21m = fwd(1, 1, a1, YM)
        to_sibling(1, 1, rows_a)
        a20p.wait_recv()
        a20m.wait_recv()
        to_sibling(2, 0, rows_a)
        b20p.wait_recv()
        b20m.wait_recv()
        z2 = fwd(2, 0, rows_b, Z)
        to_sibling(2, 0, rows_b)
        fb["z"].wait_recv()
        to_sibling(0, 1, rows_b)
        done(3, 0)
        done(1, 0)
        zm.wait_recv()
        to_sibling(3, 1, rows_b)
        done(0, 1)
        a21p.wait_recv()
        a21m.wait_recv()
        to_sibling(2, 1, rows_a)
        zp.wait_recv()
        to_sibling(1, 1, rows_b)
        done(2, 0)
        done(3, 1)
        z2.wait_recv()
        to_sibling(2, 1, rows_b)
        done(1, 1)
        done(2, 1)

    act_a = gather_a(act)
    act_b = gather_b(act)

    total0, total1 = ring_total("b", 0, b0, b1, ry_b)
    hg[gy, b0, :] = (total0 * slope[b0, :]).astype(BF16)
    hg[gy, b1, :] = (total1 * slope[b1, :]).astype(BF16)
    hg_b = gather_b(hg)
    total0, total1 = ring_total(("a", 0), 0, a0, a1, ry_a.at[0])
    z_last.wait_recv()
    hg[gy, a0, :] = ((total0 + rz_a[a0, :].astype(F32)) * slope[a0, :]).astype(BF16)
    hg[gy, a1, :] = ((total1 + rz_a[a1, :].astype(F32)) * slope[a1, :]).astype(BF16)
    hg_a = gather_a(hg)

    for copy in x_last:
        copy.wait_recv()
    xt[...] = compact(xg, FEAT).astype(BF16)
    load_wi.wait()
    acc[...] = jnp.zeros_like(acc)

    def use_hg(chip):
        k = len(stored)
        pair = pl.ds(chip * 2, 2)
        columns = pl.ds(pl.multiple_of(chip * 2 * UNITS, 2 * UNITS), 2 * UNITS)

        def tile(i, carry):
            rows = pl.ds(pl.multiple_of(i * 128, 128), 128)
            block = hg[pair].reshape(2 * UNITS, LIVE)
            acc[rows, :] += dot(wi[rows, columns], block, 1, 0)
            wig[k, rows, :] = dot(xt[rows, :], block, 1, 1).astype(BF16)
            return carry

        lax.fori_loop(0, FEAT // 128, tile, 0)
        stored.append(local(wig.at[k], wi_out.at[:, columns]))

    gather_rest(hg, hg_a, hg_b, use_hg)

    accb[...] = acc[...].astype(BF16)
    in_copies = []
    for d in range(1, SHARDS):
        to = (gx + d) % SHARDS
        rows = pl.ds(pl.multiple_of(to * ROWS, ROWS), ROWS)
        in_send[d - 1] = dot(pt[rows, :], accb[...], 1, 1).astype(BF16)
        in_copies.append(send(in_send.at[d - 1], in_recv.at[d - 1], (to, gy)))

    def use_act(chip):
        k = len(stored) - 8
        pair = pl.ds(chip * 2, 2)

        def tile(i, carry):
            rows = pl.ds(pl.multiple_of(i * 128, 128), 128)
            block = act[chip * 2 + i // 2, pl.ds(pl.multiple_of((i % 2) * 128, 128), 128), :]
            wog[k, rows, :] = dot(block, dyt[...], 1, 1).astype(BF16)
            return carry

        lax.fori_loop(0, 2 * UNITS // 128, tile, 0)
        stored.append(
            local(wog.at[k], wo_out.at[pl.ds(pl.multiple_of(chip * 2 * UNITS, 2 * UNITS), 2 * UNITS)])
        )

    gather_rest(act, act_a, act_b, use_act)

    total = dot(pt[pl.ds(pl.multiple_of(gx * ROWS, ROWS), ROWS), :], accb[...], 1, 1)
    for k, copy in enumerate(in_copies):
        copy.wait_recv()
        total = total + in_recv[k].astype(F32)
    in_out[...] = total.astype(BF16)
    for copy in stored:
        copy.wait()
    for copy in sent:
        copy.wait_send()


def body(inputs, out_grad, pre_act, w_in, w_out, counts):
    vmem = pl.BlockSpec(memory_space=pltpu.VMEM)
    anywhere = pl.BlockSpec(memory_space=pl.ANY)
    qa, qb = HA // 2, HB // 2
    flops = 2 * 4 * LIVE * FEAT * UNITS * PIECES
    return pl.pallas_call(
        kernel,
        out_shape=(
            jax.ShapeDtypeStruct((ROWS, FEAT), BF16),
            jax.ShapeDtypeStruct((FEAT, PIECES * UNITS), BF16),
            jax.ShapeDtypeStruct((PIECES * UNITS, FEAT), BF16),
        ),
        in_specs=[pl.BlockSpec(memory_space=pltpu.SMEM), vmem, vmem, anywhere, anywhere, anywhere],
        out_specs=(vmem, anywhere, anywhere),
        scratch_shapes=[
            pltpu.VMEM((SHARDS * ROWS, LIVE), BF16),
            pltpu.VMEM((SHARDS, ROWS, FEAT), BF16),
            pltpu.VMEM((SHARDS, ROWS, FEAT), BF16),
            pltpu.VMEM((PIECES, SHARDS * ROWS // PIECES, UNITS), BF16),
            pltpu.VMEM((FEAT, LIVE), BF16),
            pltpu.VMEM((FEAT, LIVE), BF16),
            pltpu.VMEM((FEAT, LIVE), BF16),
            pltpu.VMEM((8, UNITS, FEAT), BF16),
            pltpu.VMEM((8, UNITS, FEAT), BF16),
            pltpu.VMEM((FEAT, PIECES * UNITS), BF16),
            pltpu.VMEM((PIECES, UNITS, LIVE), BF16),
            pltpu.VMEM((PIECES, UNITS, LIVE), BF16),
            pltpu.VMEM((UNITS, LIVE), F32),
            pltpu.VMEM((4, 2, UNITS, LIVE), F32),
            pltpu.VMEM((4, 2, UNITS, LIVE), BF16),
            pltpu.VMEM((HA, LIVE), BF16),
            pltpu.VMEM((4, HB, LIVE), BF16),
            pltpu.VMEM((2, 6, qa, LIVE), BF16),
            pltpu.VMEM((6, qb, LIVE), BF16),
            pltpu.VMEM((FEAT, LIVE), F32),
            pltpu.VMEM((FEAT, LIVE), BF16),
            pltpu.VMEM((SHARDS - 1, ROWS, FEAT), BF16),
            pltpu.VMEM((SHARDS - 1, ROWS, FEAT), BF16),
            pltpu.VMEM((8, FEAT, 2 * UNITS), BF16),
            pltpu.VMEM((8, 2 * UNITS, FEAT), BF16),
            pltpu.SemaphoreType.DMA((144,)),
            pltpu.SemaphoreType.DMA((144,)),
            pltpu.SemaphoreType.DMA((20,)),
        ],
        compiler_params=pltpu.CompilerParams(
            collective_id=0, has_side_effects=True, vmem_limit_bytes=60 * 1024 * 1024
        ),
        cost_estimate=pl.CostEstimate(flops=flops, bytes_accessed=16 << 20, transcendentals=UNITS * LIVE),
        name="ffn_backward",
    )(counts, inputs, out_grad, pre_act, w_in, w_out.reshape(8, 2, UNITS, FEAT))


def solution(mesh):
    return jax.shard_map(
        body,
        mesh=mesh,
        in_specs=(P("gx", "gy"), P("gx", "gy"), P("gy", "gx"), P("gy", "gx"), P("gx", "gy"), P()),
        out_specs=(P("gx", "gy"), P("gy", "gx"), P("gx", "gy")),
        check_vma=False,
    )
```

time: 427 us -> 129 us (0.30)
  waiting for transfers between devices: 353 us -> 0 us
  Pallas kernels: 0 us -> 120 us
  matrix products: 35.9 us -> 0 us
  blocking collectives: 17.3 us -> 0 us
  between operations: 14.1 us -> 0.64 us
  local copies, waits for them, and re-layouts: 1.28 us -> 8.43 us
    all_gather x4 -> x0, waiting for transfers between devices: 180 us -> none  [the longest x1 50.6 us: body(): live_dy = compact(lax.all_gather(out_grad, 'gx', axis=0, tiled=True))]
    reduce_scatter x2 -> x0, waiting for transfers between devices: 171 us -> none  [the longest x1 103 us: body(): lax.psum_scatter(contract_last(live_dy, w_out), 'gy', scatter_dimension=1...]
    pallas_call x0 -> x1, Pallas kernels: none -> 120 us  [body(): pl.pallas_call(kernel, out_shape=(jax.ShapeDtypeStruct((ROWS, FEAT), BF16...]
    dot_general x6 -> x0, matrix products: 35.9 us -> none  [the longest x2 16.6 us: token_sum(): lax.dot_general(left, right, (((0,), (0,)), ((), ())), preferred_element_...]
    all_to_all x1 -> x0, blocking collectives: 17.3 us -> none  [body(): lax.all_to_all(pre_act, 'gy', split_axis=1, concat_axis=0, tiled=True)]
    unnamed x4 -> x5, local copies, waits for them, and re-layouts: 1.24 us -> 8.43 us
  transfers between devices with their start and end apart: 6 -> 0, of which waited for: 6 -> 0; matrix products, arithmetic and copies ran while one was open for 6% -> 0% of each run, Pallas kernels for 0% -> 0%
where the time goes in v2:
time: 129 us
  Pallas kernels  120 us (93%)
  local copies, waits for them, and re-layouts  8.43 us (7%)
    pallas_call x1, Pallas kernels, body(): pl.pallas_call(kernel, out_shape=(jax.ShapeDtypeStruct((ROWS, FEAT), BF16...  120 us
    unnamed x5, local copies, waits for them, and re-layouts  8.43 us

profile of v2, /device:TPU:1, one launch (start us, length us, event | category | flops | bytes accessed | tf_op | source)
XLA Modules:
  0.0 129.0 jit_solution(94868649533036152)
XLA Ops:
  0.6 120.0 %ffn_backward.1 = (bf16[128,512]{1,0:T(8,128)(2,1)}, bf16[512,4096]{1,0:T(8,128)(2,1)}, bf16[4096,512]{1,0:T(8,128)(2,1)}) custom-call(s32[8]{0:T(128)} %counts.1, bf16[128,512]{1,0:T(8,128)(2,1)} %x_ref.1, bf16[128,512]{1,0:T(8,128)(2,1)} %dy_ref.1, bf16[64,4096]{1,0:T(8,128)(2,1)} %pre_ref.1, bf16[512,4096]{1,0:T(8,128)(2,1)} %w_in_ref.1, ...), custom_call_target="tpu_custom_call" | custom-call | flops 10737418240 | bytes 16777216 | tf_op jit(solution)/shard_map/ffn_backward/pallas_call | solution.py:373
  120.6 1.6 %copy.12 = bf16[128,512]{1,0:T(8,128)(2,1)} copy(bf16[128,512]{1,0:T(8,128)(2,1)} %get-tuple-element.6) | data formatting | bytes 262144
  122.2 0.0 copy-start
  122.2 4.8 %copy.13 = bf16[512,4096]{1,0:T(8,128)(2,1)} copy(bf16[512,4096]{1,0:T(8,128)(2,1)} %get-tuple-element.7) | data formatting | bytes 8388608
  127.0 0.0 copy-done
  127.0 2.0 %copy.14 = bf16[4096,512]{1,0:T(8,128)(2,1)} copy(bf16[4096,512]{1,0:T(8,128)(2,1)S(1)} %copy-done) | data formatting | bytes 8388608
Async XLA Ops:
  122.2 4.9 %copy-start = (bf16[4096,512]{1,0:T(8,128)(2,1)S(1)}, bf16[4096,512]{1,0:T(8,128)(2,1)}, u32[]{:S(2)}) copy-start(bf16[4096,512]{1,0:T(8,128)(2,1)} %get-tuple-element.8) | copy-start | bytes 12582916

commit v3 on v2

v3 whole, which is shorter than its diff:
```python
import math

import jax
import jax.numpy as jnp
from jax import lax
from jax.experimental import pallas as pl
from jax.experimental.pallas import tpu as pltpu
from jax.sharding import PartitionSpec as P

LIVE = 640
SHARDS = 8
ROWS = 128
FEAT = 512
PIECES = 16
UNITS = 256
HA = 160
HACT = 192
HB = UNITS - HA
MESH = pl.DeviceIdType.MESH
BF16, F32 = jnp.bfloat16, jnp.float32

gelu_scale = math.sqrt(2.0 / math.pi)
cubic_coef = 0.044715


def gelu_parts(pre):
    tangent = jnp.tanh(gelu_scale * (pre + cubic_coef * pre * pre * pre))
    value = 0.5 * pre * (1.0 + tangent)
    slope = 0.5 * (1.0 + tangent) + 0.5 * pre * (1.0 - tangent * tangent) * gelu_scale * (
        1.0 + 3.0 * cubic_coef * pre * pre
    )
    return value, slope


def dot(left, right, left_dim, right_dim):
    return lax.dot_general(
        left, right, (((left_dim,), (right_dim,)), ((), ())), preferred_element_type=F32
    )


def kernel(
    counts, x_ref, dy_ref, pre_ref, w_in_ref, w_out_ref,
    in_out, wi_out, wo_out,
    pt, dyg, xg, preg, dyt, dys, xt, wo_own, wo_sib, wi, act, hg, slope,
    held, part, rz_a, rz_b, ry_a, ry_b, acc, accb, in_send, in_recv,
    send_sem, recv_sem, local_sem,
):
    gx, gy = lax.axis_index("gx"), lax.axis_index("gy")
    x, zh = gx % 4, gx // 4
    core, z, y = gy % 2, (gy // 2) % 2, gy // 4

    def on_gy(dy, dz, dc=0):
        return ((y + dy) % 4) * 4 + ((z + dz) % 2) * 2 + (core + dc) % 2

    def on_gx(dx, dzh):
        return ((zh + dzh) % 2) * 4 + (x + dx) % 4

    YP, YM, Z, C = (gx, on_gy(1, 0)), (gx, on_gy(3, 0)), (gx, on_gy(0, 1)), (gx, on_gy(0, 0, 1))
    XP, XM, ZH = (on_gx(1, 0), gy), (on_gx(3, 0), gy), (on_gx(0, 1), gy)

    count = [0, 0]
    sent = []

    def send(src, dst, device):
        k = count[0]
        count[0] += 1
        copy = pltpu.make_async_remote_copy(
            src_ref=src, dst_ref=dst, send_sem=send_sem.at[k], recv_sem=recv_sem.at[k],
            device_id=device, device_id_type=MESH,
        )
        copy.start()
        sent.append(copy)
        return copy

    def local(src, dst):
        k = count[1]
        count[1] += 1
        copy = pltpu.make_async_copy(src, dst, local_sem.at[k])
        copy.start()
        return copy

    own_pre = local(pre_ref.at[:, pl.ds(pl.multiple_of(gy * UNITS, UNITS), UNITS)], preg.at[gy])
    load_wo = local(w_out_ref.at[:, core], wo_own)
    load_wi = local(w_in_ref, wi)
    barrier = pltpu.get_barrier_semaphore()
    for d in range(1, PIECES):
        pl.semaphore_signal(barrier, inc=1, device_id=(gx, (gy + d) % PIECES), device_id_type=MESH)
    for d in range(1, SHARDS):
        pl.semaphore_signal(barrier, inc=1, device_id=((gx + d) % SHARDS, gy), device_id_type=MESH)

    pl.semaphore_wait(barrier, PIECES - 1 + SHARDS - 1)

    lo, hi = pl.ds(0, ROWS // 2), pl.ds(ROWS // 2, ROWS // 2)

    def ring_start(src, buf):
        return send(src, buf.at[gx], ZH), send(src, buf.at[gx], XP), send(src, buf.at[gx], XM)

    def ring_relay(buf, first):
        def pass_on(dzh, to_right, to_left):
            to_right.wait_recv()
            came = on_gx(3, dzh)
            a = send(buf.at[came, lo], buf.at[came, lo], XP)
            to_left.wait_recv()
            came = on_gx(1, dzh)
            b = send(buf.at[came, hi], buf.at[came, hi], XM)
            return [a, b]

        across, right, left = first
        across.wait_recv()
        other = on_gx(0, 1)
        right2 = send(buf.at[other], buf.at[other], XP)
        left2 = send(buf.at[other], buf.at[other], XM)
        return pass_on(0, right, left) + pass_on(1, right2, left2)

    dy_first = ring_start(dy_ref, dyg)
    pre_copies = []
    for d in range(1, PIECES):
        to = (gy + d) % PIECES
        columns = pl.ds(pl.multiple_of(to * UNITS, UNITS), UNITS)
        pre_copies.append(send(pre_ref.at[:, columns], preg.at[gy], (gx, to)))
    swap_wo = send(w_out_ref.at[:, 1 - core], wo_sib, C)
    start = jnp.int32(0)
    for s in range(SHARDS):
        number = counts[s]

        def fill(i, carry, s=s, start=start, number=number):
            slot = lax.broadcasted_iota(jnp.int32, (16, LIVE), 0) + i * 16
            column = lax.broadcasted_iota(jnp.int32, (16, LIVE), 1)
            hit = (column == slot + start) & (slot < number)
            pt[pl.ds(pl.multiple_of(s * ROWS + i * 16, 16), 16), :] = jnp.where(hit, 1.0, 0.0).astype(BF16)
            return carry

        lax.fori_loop(0, ROWS // 16, fill, 0)
        start = start + number
    dyg[gx] = dy_ref[...]
    xg[gx] = x_ref[...]
    dy_last = ring_relay(dyg, dy_first)

    def compact(buf, width):
        whole = buf[...].reshape(SHARDS * ROWS, width)
        return dot(whole, pt[...], 0, 0)

    def split(ha):
        qa, qb = ha // 2, (UNITS - ha) // 2
        return (
            pl.ds(0, ha), pl.ds(ha, 2 * qb), pl.ds(0, qa), pl.ds(qa, qa), pl.ds(ha, qb), pl.ds(ha + qb, qb)
        )

    rows_a, rows_b, a0, a1, b0, b1 = split(HA)

    def gather_a(buf, ha):
        rows_a = split(ha)[0]
        own = buf.at[gy, rows_a]
        return {"z": send(own, own, Z), "+": send(own, own, YP), "-": send(own, own, YM), "c": send(own, own, C)}

    def gather_b(buf, ha):
        rows_b = split(ha)[1]
        own = buf.at[gy, rows_b]
        return {"+": send(own, own, YP), "-": send(own, own, YM), "z": send(own, own, Z), "c": send(own, own, C)}

    def gather_rest(buf, ha, fa, fb, use):
        rows_a, rows_b, a0, a1, b0, b1 = split(ha)
        sib = {(0, 0): [fa["c"], fb["c"]]}

        def fwd(dy, dz, rows, device):
            piece = buf.at[on_gy(dy, dz), rows]
            return send(piece, piece, device)

        def to_sibling(dy, dz, rows):
            sib.setdefault((dy, dz), []).append(fwd(dy, dz, rows, C))

        def done(dy, dz):
            for copy in sib[dy, dz]:
                copy.wait_recv()
            use(((y + dy) % 4) * 2 + (z + dz) % 2)

        fa["z"].wait_recv()
        plus = fwd(0, 1, rows_a, YP)
        minus = fwd(0, 1, rows_a, YM)
        to_sibling(0, 1, rows_a)
        fa["+"].wait_recv()
        a20p = fwd(3, 0, a0, YP)
        to_sibling(3, 0, rows_a)
        fa["-"].wait_recv()
        a20m = fwd(1, 0, a1, YM)
        to_sibling(1, 0, rows_a)
        fb["+"].wait_recv()
        b20p = fwd(3, 0, b0, YP)
        zm = fwd(3, 0, rows_b, Z)
        to_sibling(3, 0, rows_b)
        fb["-"].wait_recv()
        b20m = fwd(1, 0, b1, YM)
        zp = fwd(1, 0, rows_b, Z)
        to_sibling(1, 0, rows_b)
        yield
        done(0, 0)
        yield
        plus.wait_recv()
        a21p = fwd(3, 1, a0, YP)
        to_sibling(3, 1, rows_a)
        minus.wait_recv()
        a21m = fwd(1, 1, a1, YM)
        to_sibling(1, 1, rows_a)
        a20p.wait_recv()
        a20m.wait_recv()
        to_sibling(2, 0, rows_a)
        b20p.wait_recv()
        b20m.wait_recv()
        z2 = fwd(2, 0, rows_b, Z)
        to_sibling(2, 0, rows_b)
        fb["z"].wait_recv()
        to_sibling(0, 1, rows_b)
        done(3, 0)
        done(1, 0)
        zm.wait_recv()
        to_sibling(3, 1, rows_b)
        done(0, 1)
        a21p.wait_recv()
        a21m.wait_recv()
        to_sibling(2, 1, rows_a)
        zp.wait_recv()
        to_sibling(1, 1, rows_b)
        done(2, 0)
        done(3, 1)
        z2.wait_recv()
        to_sibling(2, 1, rows_b)
        done(1, 1)
        done(2, 1)
        yield

    own_pre.wait()
    for copy in pre_copies:
        copy.wait_recv()
    slope[...] = dot(preg[...].reshape(SHARDS * ROWS, UNITS), pt[...], 0, 0)

    def gelu(i, carry):
        rows = pl.ds(pl.multiple_of(i * 16, 16), 16)
        value, tilt = gelu_parts(slope[rows, :])
        act[gy, rows, :] = value.astype(BF16)
        slope[rows, :] = tilt
        return carry

    lax.fori_loop(0, UNITS // 16, gelu, 0)

    act_a = gather_a(act, HACT)
    act_b = gather_b(act, HACT)

    for copy in dy_last:
        copy.wait_recv()
    dyt[...] = compact(dyg, FEAT).astype(BF16)
    swap_dy = send(dyt, dys, C)
    x_first = ring_start(x_ref, xg)
    load_wo.wait()
    swap_wo.wait_recv()

    ring = {}

    def ring_send(key, dy, dz, q0, q1, land):
        if dy == 2:
            ring[key, "relay+"] = send(part.at[dy, dz, q0], land.at[0], YP)
            ring[key, "relay-"] = send(part.at[dy, dz, q1], land.at[1], YM)
        if dy == 1:
            ring[key, "direct+"] = send(part.at[dy, dz, q1], land.at[2], YP)
        if dy == 3:
            ring[key, "direct-"] = send(part.at[dy, dz, q0], land.at[3], YM)

    def ring_pass(key, dz, q0, q1, land):
        ring[key, "relay+"].wait_recv()
        part[1, dz, q0, :] = (held[1, dz, q0, :] + land[0].astype(F32)).astype(BF16)
        ring[key, "last+"] = send(part.at[1, dz, q0], land.at[4], YP)
        ring[key, "relay-"].wait_recv()
        part[3, dz, q1, :] = (held[3, dz, q1, :] + land[1].astype(F32)).astype(BF16)
        ring[key, "last-"] = send(part.at[3, dz, q1], land.at[5], YM)

    def ring_total(key, dz, q0, q1, land):
        ring[key, "direct-"].wait_recv()
        ring[key, "last+"].wait_recv()
        total0 = held[0, dz, q0, :] + land[3].astype(F32) + land[4].astype(F32)
        ring[key, "direct+"].wait_recv()
        ring[key, "last-"].wait_recv()
        total1 = held[0, dz, q1, :] + land[2].astype(F32) + land[5].astype(F32)
        return total0, total1

    swap_dy.wait_recv()
    z_copies = {}
    for dy, dz in ((2, 1), (2, 0), (1, 1), (3, 1), (0, 1), (1, 0), (3, 0), (0, 0)):
        chip = ((y + dy) % 4) * 2 + (z + dz) % 2
        total = dot(wo_own[chip], dyt[...], 1, 0) + dot(wo_sib[chip], dys[...], 1, 0)
        held[dy, dz] = total
        part[dy, dz] = total.astype(BF16)
        ring_send(("a", dz), dy, dz, a0, a1, ry_a.at[dz])
        if dz == 1:
            z_copies[dy] = send(part.at[dy, dz, rows_b], rz_b.at[dy], Z)

    for dz in (1, 0):
        ring_pass(("a", dz), dz, a0, a1, ry_a.at[dz])
    x_last = ring_relay(xg, x_first)
    for dy in (2, 1, 3, 0):
        z_copies[dy].wait_recv()
        total = held[dy, 0, rows_b, :] + rz_b[dy].astype(F32)
        held[dy, 0, rows_b, :] = total
        part[dy, 0, rows_b, :] = total.astype(BF16)
        ring_send("b", dy, 0, b0, b1, ry_b)
        if dy == 3:
            ring_pass("b", 0, b0, b1, ry_b)
    total0, total1 = ring_total(("a", 1), 1, a0, a1, ry_a.at[1])
    part[0, 1, a0, :] = total0.astype(BF16)
    part[0, 1, a1, :] = total1.astype(BF16)
    z_last = send(part.at[0, 1, rows_a], rz_a, Z)

    def use_act(chip):
        block = act[pl.ds(chip * 2, 2)].reshape(2 * UNITS, LIVE)
        wo_out[chip] = dot(block, dyt[...], 1, 1).astype(BF16)

    act_steps = gather_rest(act, HACT, act_a, act_b, use_act)
    next(act_steps)

    total0, total1 = ring_total("b", 0, b0, b1, ry_b)
    hg[gy, b0, :] = (total0 * slope[b0, :]).astype(BF16)
    hg[gy, b1, :] = (total1 * slope[b1, :]).astype(BF16)
    hg_b = gather_b(hg, HA)
    total0, total1 = ring_total(("a", 0), 0, a0, a1, ry_a.at[0])
    z_last.wait_recv()
    hg[gy, a0, :] = ((total0 + rz_a[a0, :].astype(F32)) * slope[a0, :]).astype(BF16)
    hg[gy, a1, :] = ((total1 + rz_a[a1, :].astype(F32)) * slope[a1, :]).astype(BF16)
    hg_a = gather_a(hg, HA)

    next(act_steps)
    for copy in x_last:
        copy.wait_recv()
    xt[...] = compact(xg, FEAT).astype(BF16)
    load_wi.wait()
    acc[...] = jnp.zeros_like(acc)

    def use_hg(chip):
        columns = pl.ds(pl.multiple_of(chip * 2 * UNITS, 2 * UNITS), 2 * UNITS)
        block = hg[pl.ds(chip * 2, 2)].reshape(2 * UNITS, LIVE)
        acc[...] += dot(wi[:, columns], block, 1, 0)
        wi_out[chip] = dot(xt[...], block, 1, 1).astype(BF16)

    for _ in gather_rest(hg, HA, hg_a, hg_b, use_hg):
        pass

    accb[...] = acc[...].astype(BF16)
    in_copies = []
    for d in range(1, SHARDS):
        to = (gx + d) % SHARDS
        rows = pl.ds(pl.multiple_of(to * ROWS, ROWS), ROWS)
        in_send[d - 1] = dot(pt[rows, :], accb[...], 1, 1).astype(BF16)
        in_copies.append(send(in_send.at[d - 1], in_recv.at[d - 1], (to, gy)))

    for _ in act_steps:
        pass

    total = dot(pt[pl.ds(pl.multiple_of(gx * ROWS, ROWS), ROWS), :], accb[...], 1, 1)
    for k, copy in enumerate(in_copies):
        copy.wait_recv()
        total = total + in_recv[k].astype(F32)
    in_out[...] = total.astype(BF16)
    for copy in sent:
        copy.wait_send()


def store_kernel(in_ref, wi_ref, wo_ref, in_out, wi_out, wo_out, sem):
    copies = [pltpu.make_async_copy(in_ref, in_out, sem.at[16])]
    for chip in range(8):
        span = pl.ds(chip * 2 * UNITS, 2 * UNITS)
        copies.append(pltpu.make_async_copy(wi_ref.at[chip], wi_out.at[:, span], sem.at[chip]))
        copies.append(pltpu.make_async_copy(wo_ref.at[chip], wo_out.at[span], sem.at[8 + chip]))
    for copy in copies:
        copy.start()
    for copy in copies:
        copy.wait()


def body(inputs, out_grad, pre_act, w_in, w_out, counts):
    vmem = pl.BlockSpec(memory_space=pltpu.VMEM)
    anywhere = pl.BlockSpec(memory_space=pl.ANY)
    qa, qb = HA // 2, HB // 2
    flops = 2 * 4 * LIVE * FEAT * UNITS * PIECES
    results = pl.pallas_call(
        kernel,
        out_shape=(
            pltpu.VMEM((ROWS, FEAT), BF16),
            pltpu.VMEM((8, FEAT, 2 * UNITS), BF16),
            pltpu.VMEM((8, 2 * UNITS, FEAT), BF16),
        ),
        in_specs=[pl.BlockSpec(memory_space=pltpu.SMEM), vmem, vmem, anywhere, anywhere, anywhere],
        out_specs=(vmem, vmem, vmem),
        scratch_shapes=[
            pltpu.VMEM((SHARDS * ROWS, LIVE), BF16),
            pltpu.VMEM((SHARDS, ROWS, FEAT), BF16),
            pltpu.VMEM((SHARDS, ROWS, FEAT), BF16),
            pltpu.VMEM((PIECES, SHARDS * ROWS // PIECES, UNITS), BF16),
            pltpu.VMEM((FEAT, LIVE), BF16),
            pltpu.VMEM((FEAT, LIVE), BF16),
            pltpu.VMEM((FEAT, LIVE), BF16),
            pltpu.VMEM((8, UNITS, FEAT), BF16),
            pltpu.VMEM((8, UNITS, FEAT), BF16),
            pltpu.VMEM((FEAT, PIECES * UNITS), BF16),
            pltpu.VMEM((PIECES, UNITS, LIVE), BF16),
            pltpu.VMEM((PIECES, UNITS, LIVE), BF16),
            pltpu.VMEM((UNITS, LIVE), F32),
            pltpu.VMEM((4, 2, UNITS, LIVE), F32),
            pltpu.VMEM((4, 2, UNITS, LIVE), BF16),
            pltpu.VMEM((HA, LIVE), BF16),
            pltpu.VMEM((4, HB, LIVE), BF16),
            pltpu.VMEM((2, 6, qa, LIVE), BF16),
            pltpu.VMEM((6, qb, LIVE), BF16),
            pltpu.VMEM((FEAT, LIVE), F32),
            pltpu.VMEM((FEAT, LIVE), BF16),
            pltpu.VMEM((SHARDS - 1, ROWS, FEAT), BF16),
            pltpu.VMEM((SHARDS - 1, ROWS, FEAT), BF16),
            pltpu.SemaphoreType.DMA((144,)),
            pltpu.SemaphoreType.DMA((144,)),
            pltpu.SemaphoreType.DMA((3,)),
        ],
        compiler_params=pltpu.CompilerParams(
            collective_id=0, has_side_effects=True, vmem_limit_bytes=48 * 1024 * 1024
        ),
        cost_estimate=pl.CostEstimate(flops=flops, bytes_accessed=16 << 20, transcendentals=UNITS * LIVE),
        name="ffn_backward",
    )(counts, inputs, out_grad, pre_act, w_in, w_out.reshape(8, 2, UNITS, FEAT))
    return pl.pallas_call(
        store_kernel,
        out_shape=(
            jax.ShapeDtypeStruct((ROWS, FEAT), BF16),
            jax.ShapeDtypeStruct((FEAT, PIECES * UNITS), BF16),
            jax.ShapeDtypeStruct((PIECES * UNITS, FEAT), BF16),
        ),
        in_specs=[vmem, vmem, vmem],
        out_specs=(anywhere, anywhere, anywhere),
        scratch_shapes=[pltpu.SemaphoreType.DMA((17,))],
        compiler_params=pltpu.CompilerParams(vmem_limit_bytes=16 * 1024 * 1024),
        name="store_results",
    )(*results)


def solution(mesh):
    return jax.shard_map(
        body,
        mesh=mesh,
        in_specs=(P("gx", "gy"), P("gx", "gy"), P("gy", "gx"), P("gy", "gx"), P("gx", "gy"), P()),
        out_specs=(P("gx", "gy"), P("gy", "gx"), P("gx", "gy")),
        check_vma=False,
    )
```

time: 129 us -> 109 us (0.84)
  Pallas kernels: 120 us -> 108 us
  local copies, waits for them, and re-layouts: 8.43 us -> 0 us
    pallas_call x1 -> x2, Pallas kernels: 120 us -> 108 us  [the longest x1 104 us: body(): pl.pallas_call(kernel, out_shape=(pltpu.VMEM((ROWS, FEAT), BF16), pltpu.V...]
    unnamed x5 -> x0, local copies, waits for them, and re-layouts: 8.43 us -> none
where the time goes in v3:
time: 109 us
  Pallas kernels  108 us (99%)
    pallas_call x1, Pallas kernels, body(): pl.pallas_call(kernel, out_shape=(pltpu.VMEM((ROWS, FEAT), BF16), pltpu.V...  104 us
    pallas_call x1, Pallas kernels, body(): pl.pallas_call(store_kernel, out_shape=(jax.ShapeDtypeStruct((ROWS, FEAT)...  3.47 us

profile of v3, /device:TPU:1, one launch (start us, length us, event | category | flops | bytes accessed | tf_op | source)
XLA Modules:
  0.0 108.7 jit_solution(18036788277130230847)
XLA Ops:
  0.6 104.4 %ffn_backward.1 = (bf16[128,512]{1,0:T(8,128)(2,1)S(1)}, bf16[8,512,512]{2,1,0:T(8,128)(2,1)S(1)}, bf16[8,512,512]{2,1,0:T(8,128)(2,1)S(1)}) custom-call(s32[8]{0:T(128)} %counts.1, bf16[128,512]{1,0:T(8,128)(2,1)} %x_ref.1, bf16[128,512]{1,0:T(8,128)(2,1)} %dy_ref.1, bf16[64,4096]{1,0:T(8,128)(2,1)} %pre_ref.1, bf16[512,4096]{1,0:T(8,128)(2,1)} %w_in_ref.1, ...), custom_call_target="tpu_custom_call" | custom-call | flops 10737418240 | bytes 16777216 | tf_op jit(solution)/shard_map/ffn_backward/pallas_call | solution.py:381
  105.0 3.5 %store_results.1 = (bf16[128,512]{1,0:T(8,128)(2,1)}, bf16[512,4096]{1,0:T(8,128)(2,1)}, bf16[4096,512]{1,0:T(8,128)(2,1)}) custom-call(bf16[128,512]{1,0:T(8,128)(2,1)S(1)} %get-tuple-element.6.in_ref, bf16[8,512,512]{2,1,0:T(8,128)(2,1)S(1)} %get-tuple-element.7.wi_ref, bf16[8,512,512]{2,1,0:T(8,128)(2,1)S(1)} %get-tuple-element.8.wo_ref), custom_call_target="tpu_custom_call" | custom-call | tf_op jit(solution)/shard_map/store_results/pallas_call | solution.py:424

commit v4 on v3

--- a/solution.py
+++ b/solution.py
@@ -42,7 +42,7 @@
     counts, x_ref, dy_ref, pre_ref, w_in_ref, w_out_ref,
     in_out, wi_out, wo_out,
     pt, dyg, xg, preg, dyt, dys, xt, wo_own, wo_sib, wi, act, hg, slope,
-    held, part, rz_a, rz_b, ry_a, ry_b, acc, accb, in_send, in_recv,
+    held, part, rz_a, rz_b, ry_a, ry_b, acc, accb, left_part, right_part, left_x, left_send, left_z, right_z, right_send, right_x,
     send_sem, recv_sem, local_sem,
 ):
     gx, gy = lax.axis_index("gx"), lax.axis_index("gy")
@@ -80,6 +80,7 @@
         return copy
 
     own_pre = local(pre_ref.at[:, pl.ds(pl.multiple_of(gy * UNITS, UNITS), UNITS)], preg.at[gy])
+    own_dy, own_x = local(dy_ref, dyg.at[gx]), local(x_ref, xg.at[gx])
     load_wo = local(w_out_ref.at[:, core], wo_own)
     load_wi = local(w_in_ref, wi)
     barrier = pltpu.get_barrier_semaphore()
@@ -132,8 +133,6 @@
 
         lax.fori_loop(0, ROWS // 16, fill, 0)
         start = start + number
-    dyg[gx] = dy_ref[...]
-    xg[gx] = x_ref[...]
     dy_last = ring_relay(dyg, dy_first)
 
     def compact(buf, width):
@@ -212,6 +211,7 @@
         to_sibling(0, 1, rows_b)
         done(3, 0)
         done(1, 0)
+        yield
         zm.wait_recv()
         to_sibling(3, 1, rows_b)
         done(0, 1)
@@ -247,6 +247,7 @@
 
     for copy in dy_last:
         copy.wait_recv()
+    own_dy.wait()
     dyt[...] = compact(dyg, FEAT).astype(BF16)
     swap_dy = send(dyt, dys, C)
     x_first = ring_start(x_ref, xg)
@@ -328,35 +329,70 @@
     next(act_steps)
     for copy in x_last:
         copy.wait_recv()
+    own_x.wait()
     xt[...] = compact(xg, FEAT).astype(BF16)
     load_wi.wait()
     acc[...] = jnp.zeros_like(acc)
 
+    late = []
+
+    def block_of(buf, chip):
+        return buf[pl.ds(chip * 2, 2)].reshape(2 * UNITS, LIVE)
+
     def use_hg(chip):
         columns = pl.ds(pl.multiple_of(chip * 2 * UNITS, 2 * UNITS), 2 * UNITS)
-        block = hg[pl.ds(chip * 2, 2)].reshape(2 * UNITS, LIVE)
+        block = block_of(hg, chip)
         acc[...] += dot(wi[:, columns], block, 1, 0)
-        wi_out[chip] = dot(xt[...], block, 1, 1).astype(BF16)
-
-    for _ in gather_rest(hg, HA, hg_a, hg_b, use_hg):
-        pass
-
+        late.append(chip)
+        if len(late) <= 4:
+            wi_out[chip] = dot(xt[...], block, 1, 1).astype(BF16)
+
+    hg_steps = gather_rest(hg, HA, hg_a, hg_b, use_hg)
+    for _ in range(3):
+        next(hg_steps)
+    next(act_steps)
+    next(hg_steps)
+
+    half = FEAT // 2
     accb[...] = acc[...].astype(BF16)
-    in_copies = []
-    for d in range(1, SHARDS):
-        to = (gx + d) % SHARDS
-        rows = pl.ds(pl.multiple_of(to * ROWS, ROWS), ROWS)
-        in_send[d - 1] = dot(pt[rows, :], accb[...], 1, 1).astype(BF16)
-        in_copies.append(send(in_send.at[d - 1], in_recv.at[d - 1], (to, gy)))
+    right_part[...] = dot(pt[...], accb[half:, :], 1, 1).astype(BF16).reshape(SHARDS, ROWS, half)
+    far = pl.ds((1 - zh) * 4, 4)
+    right_copy = send(right_part.at[far], right_z, ZH)
+    left_part[...] = dot(pt[...], accb[:half, :], 1, 1).astype(BF16).reshape(SHARDS, ROWS, half)
+    left_copies = [
+        send(left_part.at[on_gx(d, dzh)], left_x.at[dzh, d - 1], (on_gx(d, 0), gy))
+        for dzh in (1, 0) for d in (1, 2, 3)
+    ]
+    for chip in late[4:]:
+        wi_out[chip] = dot(xt[...], block_of(hg, chip), 1, 1).astype(BF16)
+    right_copy.wait_recv()
+    right_last = []
+    for d in (2, 1, 3):
+        right_send[d - 1] = (
+            right_part[on_gx(d, 0)].astype(F32) + right_z[(x + d) % 4].astype(F32)
+        ).astype(BF16)
+        right_last.append(send(right_send.at[d - 1], right_x.at[d - 1], (on_gx(d, 0), gy)))
+    for copy in left_copies[:3]:
+        copy.wait_recv()
+    total = left_part[on_gx(0, 1)].astype(F32)
+    for d in range(3):
+        total = total + left_x[1, d].astype(F32)
+    left_send[...] = total.astype(BF16)
+    left_last = send(left_send, left_z, ZH)
 
     for _ in act_steps:
         pass
 
-    total = dot(pt[pl.ds(pl.multiple_of(gx * ROWS, ROWS), ROWS), :], accb[...], 1, 1)
-    for k, copy in enumerate(in_copies):
+    for copy in left_copies[3:] + right_last + [left_last]:
         copy.wait_recv()
-        total = total + in_recv[k].astype(F32)
-    in_out[...] = total.astype(BF16)
+    total = left_part[gx].astype(F32) + left_z[...].astype(F32)
+    for d in range(3):
+        total = total + left_x[0, d].astype(F32)
+    in_out[:, :half] = total.astype(BF16)
+    total = right_part[gx].astype(F32) + right_z[x].astype(F32)
+    for d in range(3):
+        total = total + right_x[d].astype(F32)
+    in_out[:, half:] = total.astype(BF16)
     for copy in sent:
         copy.wait_send()
 
@@ -385,7 +421,7 @@
             pltpu.VMEM((8, FEAT, 2 * UNITS), BF16),
             pltpu.VMEM((8, 2 * UNITS, FEAT), BF16),
         ),
-        in_specs=[pl.BlockSpec(memory_space=pltpu.SMEM), vmem, vmem, anywhere, anywhere, anywhere],
+        in_specs=[pl.BlockSpec(memory_space=pltpu.SMEM)] + [anywhere] * 5,
         out_specs=(vmem, vmem, vmem),
         scratch_shapes=[
             pltpu.VMEM((SHARDS * ROWS, LIVE), BF16),
@@ -409,11 +445,17 @@
             pltpu.VMEM((6, qb, LIVE), BF16),
             pltpu.VMEM((FEAT, LIVE), F32),
             pltpu.VMEM((FEAT, LIVE), BF16),
-            pltpu.VMEM((SHARDS - 1, ROWS, FEAT), BF16),
-            pltpu.VMEM((SHARDS - 1, ROWS, FEAT), BF16),
+            pltpu.VMEM((SHARDS, ROWS, FEAT // 2), BF16),
+            pltpu.VMEM((SHARDS, ROWS, FEAT // 2), BF16),
+            pltpu.VMEM((2, 3, ROWS, FEAT // 2), BF16),
+            pltpu.VMEM((ROWS, FEAT // 2), BF16),
+            pltpu.VMEM((ROWS, FEAT // 2), BF16),
+            pltpu.VMEM((4, ROWS, FEAT // 2), BF16),
+            pltpu.VMEM((3, ROWS, FEAT // 2), BF16),
+            pltpu.VMEM((3, ROWS, FEAT // 2), BF16),
             pltpu.SemaphoreType.DMA((144,)),
             pltpu.SemaphoreType.DMA((144,)),
-            pltpu.SemaphoreType.DMA((3,)),
+            pltpu.SemaphoreType.DMA((5,)),
         ],
         compiler_params=pltpu.CompilerParams(
             collective_id=0, has_side_effects=True, vmem_limit_bytes=48 * 1024 * 1024

time: 109 us -> 105 us (0.963)
  Pallas kernels: 108 us -> 104 us
    pallas_call x1, Pallas kernels: 104 us -> 100 us  [body(): pl.pallas_call(kernel, out_shape=(pltpu.VMEM((ROWS, FEAT), BF16), pltpu.V...]
where the time goes in v4:
time: 105 us
  Pallas kernels  104 us (99%)
    pallas_call x1, Pallas kernels, body(): pl.pallas_call(kernel, out_shape=(pltpu.VMEM((ROWS, FEAT), BF16), pltpu.V...  100 us
    pallas_call x1, Pallas kernels, body(): pl.pallas_call(store_kernel, out_shape=(jax.ShapeDtypeStruct((ROWS, FEAT)...  3.47 us

profile of v4, /device:TPU:1, one launch (start us, length us, event | category | flops | bytes accessed | tf_op | source)
XLA Modules:
  0.0 104.7 jit_solution(15309175903744127383)
XLA Ops:
  0.6 100.4 %ffn_backward.1 = (bf16[128,512]{1,0:T(8,128)(2,1)S(1)}, bf16[8,512,512]{2,1,0:T(8,128)(2,1)S(1)}, bf16[8,512,512]{2,1,0:T(8,128)(2,1)S(1)}) custom-call(s32[8]{0:T(128)} %counts.1, bf16[128,512]{1,0:T(8,128)(2,1)} %x_ref.1, bf16[128,512]{1,0:T(8,128)(2,1)} %dy_ref.1, bf16[64,4096]{1,0:T(8,128)(2,1)} %pre_ref.1, bf16[512,4096]{1,0:T(8,128)(2,1)} %w_in_ref.1, ...), custom_call_target="tpu_custom_call" | custom-call | flops 10737418240 | bytes 16777216 | tf_op jit(solution)/shard_map/ffn_backward/pallas_call | solution.py:417
  101.0 3.5 %store_results.1 = (bf16[128,512]{1,0:T(8,128)(2,1)}, bf16[512,4096]{1,0:T(8,128)(2,1)}, bf16[4096,512]{1,0:T(8,128)(2,1)}) custom-call(bf16[128,512]{1,0:T(8,128)(2,1)S(1)} %get-tuple-element.6.in_ref, bf16[8,512,512]{2,1,0:T(8,128)(2,1)S(1)} %get-tuple-element.7.wi_ref, bf16[8,512,512]{2,1,0:T(8,128)(2,1)S(1)} %get-tuple-element.8.wo_ref), custom_call_target="tpu_custom_call" | custom-call | tf_op jit(solution)/shard_map/store_results/pallas_call | solution.py:466

commit v5 on v4

--- a/solution.py
+++ b/solution.py
@@ -91,29 +91,35 @@
 
     pl.semaphore_wait(barrier, PIECES - 1 + SHARDS - 1)
 
-    lo, hi = pl.ds(0, ROWS // 2), pl.ds(ROWS // 2, ROWS // 2)
-
-    def ring_start(src, buf):
-        return send(src, buf.at[gx], ZH), send(src, buf.at[gx], XP), send(src, buf.at[gx], XM)
+    def ring_start(src, buf, chunks):
+        size = ROWS // chunks
+        return [
+            [send(src.at[pl.ds(k * size, size)], buf.at[gx, pl.ds(k * size, size)], to) for to in (ZH, XP, XM)]
+            for k in range(chunks)
+        ]
 
     def ring_relay(buf, first):
-        def pass_on(dzh, to_right, to_left):
+        size = ROWS // len(first)
+        last, second = [], []
+
+        def pass_on(k, dzh, to_right, to_left):
             to_right.wait_recv()
-            came = on_gx(3, dzh)
-            a = send(buf.at[came, lo], buf.at[came, lo], XP)
+            piece = buf.at[on_gx(3, dzh), pl.ds(k * size, size // 2)]
+            last.append(send(piece, piece, XP))
             to_left.wait_recv()
-            came = on_gx(1, dzh)
-            b = send(buf.at[came, hi], buf.at[came, hi], XM)
-            return [a, b]
-
-        across, right, left = first
-        across.wait_recv()
-        other = on_gx(0, 1)
-        right2 = send(buf.at[other], buf.at[other], XP)
-        left2 = send(buf.at[other], buf.at[other], XM)
-        return pass_on(0, right, left) + pass_on(1, right2, left2)
-
-    dy_first = ring_start(dy_ref, dyg)
+            piece = buf.at[on_gx(1, dzh), pl.ds(k * size + size // 2, size // 2)]
+            last.append(send(piece, piece, XM))
+
+        for k, (across, right, left) in enumerate(first):
+            across.wait_recv()
+            piece = buf.at[on_gx(0, 1), pl.ds(k * size, size)]
+            second.append((send(piece, piece, XP), send(piece, piece, XM)))
+            pass_on(k, 0, right, left)
+        for k, (right, left) in enumerate(second):
+            pass_on(k, 1, right, left)
+        return last
+
+    dy_first = ring_start(dy_ref, dyg, 2)
     pre_copies = []
     for d in range(1, PIECES):
         to = (gy + d) % PIECES
@@ -250,7 +256,7 @@
     own_dy.wait()
     dyt[...] = compact(dyg, FEAT).astype(BF16)
     swap_dy = send(dyt, dys, C)
-    x_first = ring_start(x_ref, xg)
+    x_first = ring_start(x_ref, xg, 1)
     load_wo.wait()
     swap_wo.wait_recv()
 
@@ -282,11 +288,13 @@
         total1 = held[0, dz, q1, :] + land[2].astype(F32) + land[5].astype(F32)
         return total0, total1
 
-    swap_dy.wait_recv()
     z_copies = {}
     for dy, dz in ((2, 1), (2, 0), (1, 1), (3, 1), (0, 1), (1, 0), (3, 0), (0, 0)):
         chip = ((y + dy) % 4) * 2 + (z + dz) % 2
-        total = dot(wo_own[chip], dyt[...], 1, 0) + dot(wo_sib[chip], dys[...], 1, 0)
+        total = dot(wo_own[chip], dyt[...], 1, 0)
+        if (dy, dz) == (2, 1):
+            swap_dy.wait_recv()
+        total = total + dot(wo_sib[chip], dys[...], 1, 0)
         held[dy, dz] = total
         part[dy, dz] = total.astype(BF16)
         ring_send(("a", dz), dy, dz, a0, a1, ry_a.at[dz])
@@ -453,8 +461,8 @@
             pltpu.VMEM((4, ROWS, FEAT // 2), BF16),
             pltpu.VMEM((3, ROWS, FEAT // 2), BF16),
             pltpu.VMEM((3, ROWS, FEAT // 2), BF16),
-            pltpu.SemaphoreType.DMA((144,)),
-            pltpu.SemaphoreType.DMA((144,)),
+            pltpu.SemaphoreType.DMA((152,)),
+            pltpu.SemaphoreType.DMA((152,)),
             pltpu.SemaphoreType.DMA((5,)),
         ],
         compiler_params=pltpu.CompilerParams(

time: 105 us -> 104 us (level)
  no operation moved by 1% of the time
where the time goes in v5:
time: 104 us
  Pallas kernels  103 us (99%)
    pallas_call x1, Pallas kernels, body(): pl.pallas_call(kernel, out_shape=(pltpu.VMEM((ROWS, FEAT), BF16), pltpu.V...  99.9 us
    pallas_call x1, Pallas kernels, body(): pl.pallas_call(store_kernel, out_shape=(jax.ShapeDtypeStruct((ROWS, FEAT)...  3.47 us

profile of v5, /device:TPU:1, one launch (start us, length us, event | category | flops | bytes accessed | tf_op | source)
XLA Modules:
  0.0 104.2 jit_solution(3634247911728793208)
XLA Ops:
  0.6 99.9 %ffn_backward.1 = (bf16[128,512]{1,0:T(8,128)(2,1)S(1)}, bf16[8,512,512]{2,1,0:T(8,128)(2,1)S(1)}, bf16[8,512,512]{2,1,0:T(8,128)(2,1)S(1)}) custom-call(s32[8]{0:T(128)} %counts.1, bf16[128,512]{1,0:T(8,128)(2,1)} %x_ref.1, bf16[128,512]{1,0:T(8,128)(2,1)} %dy_ref.1, bf16[64,4096]{1,0:T(8,128)(2,1)} %pre_ref.1, bf16[512,4096]{1,0:T(8,128)(2,1)} %w_in_ref.1, ...), custom_call_target="tpu_custom_call" | custom-call | flops 10737418240 | bytes 16777216 | tf_op jit(solution)/shard_map/ffn_backward/pallas_call | solution.py:425
  100.5 3.5 %store_results.1 = (bf16[128,512]{1,0:T(8,128)(2,1)}, bf16[512,4096]{1,0:T(8,128)(2,1)}, bf16[4096,512]{1,0:T(8,128)(2,1)}) custom-call(bf16[128,512]{1,0:T(8,128)(2,1)S(1)} %get-tuple-element.6.in_ref, bf16[8,512,512]{2,1,0:T(8,128)(2,1)S(1)} %get-tuple-element.7.wi_ref, bf16[8,512,512]{2,1,0:T(8,128)(2,1)S(1)} %get-tuple-element.8.wo_ref), custom_call_target="tpu_custom_call" | custom-call | tf_op jit(solution)/shard_map/store_results/pallas_call | solution.py:474

commit v6 on v5

--- a/solution.py
+++ b/solution.py
@@ -303,7 +303,6 @@
 
     for dz in (1, 0):
         ring_pass(("a", dz), dz, a0, a1, ry_a.at[dz])
-    x_last = ring_relay(xg, x_first)
     for dy in (2, 1, 3, 0):
         z_copies[dy].wait_recv()
         total = held[dy, 0, rows_b, :] + rz_b[dy].astype(F32)
@@ -312,6 +311,7 @@
         ring_send("b", dy, 0, b0, b1, ry_b)
         if dy == 3:
             ring_pass("b", 0, b0, b1, ry_b)
+    x_last = ring_relay(xg, x_first)
     total0, total1 = ring_total(("a", 1), 1, a0, a1, ry_a.at[1])
     part[0, 1, a0, :] = total0.astype(BF16)
     part[0, 1, a1, :] = total1.astype(BF16)

time: 104 us -> 109 us (1.048); the launches traced: 104 us -> 107 us
  Pallas kernels: 103 us -> 106 us
    pallas_call x1, Pallas kernels: 99.9 us -> 102 us  [body(): pl.pallas_call(kernel, out_shape=(pltpu.VMEM((ROWS, FEAT), BF16), pltpu.V...]
where the time goes in v6:
time: 109 us; the launch traced here: 107 us
  Pallas kernels  106 us (97%)
    pallas_call x1, Pallas kernels, body(): pl.pallas_call(kernel, out_shape=(pltpu.VMEM((ROWS, FEAT), BF16), pltpu.V...  102 us
    pallas_call x1, Pallas kernels, body(): pl.pallas_call(store_kernel, out_shape=(jax.ShapeDtypeStruct((ROWS, FEAT)...  3.47 us

profile of v6, /device:TPU:1, one launch (start us, length us, event | category | flops | bytes accessed | tf_op | source)
XLA Modules:
  0.0 106.6 jit_solution(2670978595012836746)
XLA Ops:
  0.6 102.3 %ffn_backward.1 = (bf16[128,512]{1,0:T(8,128)(2,1)S(1)}, bf16[8,512,512]{2,1,0:T(8,128)(2,1)S(1)}, bf16[8,512,512]{2,1,0:T(8,128)(2,1)S(1)}) custom-call(s32[8]{0:T(128)} %counts.1, bf16[128,512]{1,0:T(8,128)(2,1)} %x_ref.1, bf16[128,512]{1,0:T(8,128)(2,1)} %dy_ref.1, bf16[64,4096]{1,0:T(8,128)(2,1)} %pre_ref.1, bf16[512,4096]{1,0:T(8,128)(2,1)} %w_in_ref.1, ...), custom_call_target="tpu_custom_call" | custom-call | flops 10737418240 | bytes 16777216 | tf_op jit(solution)/shard_map/ffn_backward/pallas_call | solution.py:425
  103.0 3.5 %store_results.1 = (bf16[128,512]{1,0:T(8,128)(2,1)}, bf16[512,4096]{1,0:T(8,128)(2,1)}, bf16[4096,512]{1,0:T(8,128)(2,1)}) custom-call(bf16[128,512]{1,0:T(8,128)(2,1)S(1)} %get-tuple-element.6.in_ref, bf16[8,512,512]{2,1,0:T(8,128)(2,1)S(1)} %get-tuple-element.7.wi_ref, bf16[8,512,512]{2,1,0:T(8,128)(2,1)S(1)} %get-tuple-element.8.wo_ref), custom_call_target="tpu_custom_call" | custom-call | tf_op jit(solution)/shard_map/store_results/pallas_call | solution.py:474
